TPU v7x, 512 devices: a whole 4x8x8 slice. The times are simulated.
512 devices in a mesh: dp: 8 (over z), tensor: 4 (over y_lo, core), grid: 16 (over y_hi, x).
Axes of the slice: x: 4, y: 8 (y_hi: 4, y_lo: 2; y = y_hi * 2 + y_lo), z: 8, core: 2. Of those that a mesh axis runs over, the one named last changes fastest.
Arguments:
- tokens: bfloat16 [6144, 8192], P('dp', 'grid'), may hold values from -6 to 6
- cotangents: bfloat16 [2, 6144, 1024], P(None, 'dp', 'tensor'), may hold values from -0.015625 to 0.015625
- left_stat: float32 [2, 8192, 8192], P(None, ('dp', 'tensor'), 'grid'), may hold values from -6 to 6
- right_stat: float32 [2, 1024, 1024], P(None, ('dp', 'tensor'), 'grid'), may hold values from -6 to 6
- left_root: bfloat16 [2, 8192, 8192], P(None, ('dp', 'tensor'), 'grid'), may hold values from -0.3125 to 0.3125
- right_root: bfloat16 [2, 1024, 1024], P(None, 'grid'), as said below
- momentum: float32 [2, 8192, 1024], P(None, ('dp', 'tensor', 'grid')), may hold values from -6 to 6
Outputs:
- new_left: float32 [2, 8192, 8192], P(None, ('dp', 'tensor'), 'grid')
- new_right: float32 [2, 1024, 1024], P(None, ('dp', 'tensor'), 'grid')
- new_momentum: float32 [2, 8192, 1024], P(None, ('dp', 'tensor', 'grid'))
Inputs may be any that keep to these rules, and one draw needn't show every extreme that they name: `right_root`: each of the two factors is exactly symmetric.
All inputs are finite; a program needn't handle non-finite values.
Results may differ from a plain program's by a relative error of at most 0.0023.
Values may be sent and summed in bfloat16 or wider, within the bound.
A program may use at most 64 MiB of HBM per device.

v0:
```python
import jax
import jax.numpy as jnp
from jax import lax
from jax.sharding import PartitionSpec as P

stat_decay = 0.9
momentum_decay = 0.9


def in_blocks(shard, dim, size):
    dims = shard.shape
    pieces = shard.reshape(*dims[:dim], size, dims[dim] // size, *dims[dim + 1 :])
    return jnp.moveaxis(pieces, dim, 0)


def sum_at_owner(shard, axis, dim):
    size = lax.axis_size(axis)
    pieces = lax.all_to_all(in_blocks(shard, dim, size), axis, 0, 0, tiled=True)
    return jnp.sum(pieces, axis=0)


def rows_for(lines, size):
    spare = -lines.shape[0] % size
    if not spare:
        return lines
    return jnp.concatenate([lines, jnp.zeros((spare, *lines.shape[1:]), lines.dtype)])


def spread(shard, axis, root):
    lines = jnp.where(lax.axis_index(axis) == root, shard, jnp.zeros_like(shard)).reshape(
        -1, *shard.shape[1:][-1:]
    )
    padded = rows_for(lines, lax.axis_size(axis))
    own = lax.psum_scatter(padded, axis, scatter_dimension=0, tiled=True)
    return lax.all_gather(own, axis, axis=0, tiled=True)[: len(lines)].reshape(shard.shape)


def shards(tokens, cotangents, left_stat, right_stat, left_root, right_root, momentum):
    partial_grad = jnp.einsum("tr,pto->pro", tokens, cotangents, preferred_element_type=jnp.float32)
    shared = sum_at_owner(partial_grad, "dp", 1)
    widened = lax.all_gather(shared.astype(jnp.bfloat16), "tensor", axis=2, tiled=True)
    grad_rows = lax.all_gather(widened, "dp", axis=1, tiled=True)
    block_rows = left_stat.shape[1]
    grid_rows = left_stat.shape[2]
    learner = lax.axis_index("dp") * lax.axis_size("tensor") + lax.axis_index("tensor")
    first_row = learner * block_rows
    source = first_row // grid_rows
    offset = first_row % grid_rows
    selected = lax.dynamic_slice_in_dim(grad_rows, offset, block_rows, 1)
    own_rows = spread(selected, "grid", source)
    gram_left = jnp.einsum("pak,pbk->pab", own_rows, grad_rows, preferred_element_type=jnp.float32)
    new_left = stat_decay * left_stat + (1.0 - stat_decay) * gram_left
    column_width = right_stat.shape[2]
    column_block = lax.dynamic_slice_in_dim(
        own_rows, lax.axis_index("grid") * column_width, column_width, 2
    )
    right_term = jnp.einsum(
        "pak,pac->pkc", own_rows, column_block, preferred_element_type=jnp.float32
    )
    gram_right = sum_at_owner(right_term, ("dp", "tensor"), 1)
    new_right = stat_decay * right_stat + (1.0 - stat_decay) * gram_right
    applied = sum_at_owner(
        jnp.einsum("pab,pbk->apk", left_root, grad_rows, preferred_element_type=jnp.float32),
        "grid",
        0,
    )
    factor_local = right_root.astype(jnp.float32)
    local_columns = jnp.einsum(
        "mpk,pck->mpc",
        lax.all_gather(applied, "grid", axis=0, tiled=True),
        factor_local,
        precision=lax.Precision.HIGHEST,
        preferred_element_type=jnp.float32,
    )
    update = lax.all_to_all(local_columns, "grid", split_axis=0, concat_axis=2, tiled=True)
    new_momentum = momentum_decay * momentum + jnp.transpose(update, (1, 0, 2))
    return (new_left, new_right, new_momentum)


def solution(mesh):
    return jax.shard_map(
        shards,
        mesh=mesh,
        in_specs=(
            P("dp", "grid"),
            P(None, "dp", "tensor"),
            P(None, ("dp", "tensor"), "grid"),
            P(None, ("dp", "tensor"), "grid"),
            P(None, ("dp", "tensor"), "grid"),
            P(None, "grid", None),
            P(None, ("dp", "tensor", "grid"), None),
        ),
        out_specs=(
            P(None, ("dp", "tensor"), "grid"),
            P(None, ("dp", "tensor"), "grid"),
            P(None, ("dp", "tensor", "grid"), None),
        ),
        check_vma=False,
    )
```

profile of v0, /device:TPU:8, one launch (start us, length us, event | category | flops | bytes accessed | tf_op | source)
XLA Modules:
  0.0 374.3 jit_solution(8418410943962718748)
XLA Ops:
  7.2 1.1 copy-done
  8.3 1.7 convolution_bitcast_fusion
  10.0 0.3 copy.25
  10.5 38.8 %all_to_all.33 = f32[8,2,64,256]{3,2,1,0:T(8,128)S(1)} all-to-all(f32[8,2,64,256]{3,2,1,0:T(8,128)S(1)} %copy.26), channel_id=1, replica_groups=mesh['dp'=8,'tensor'=4,'grid'=16] {'dp'}, dimensions={0} | all-to-all | bytes 2097152 | tf_op jit(solution)/shard_map/all_to_all | solution.py:18
  49.4 6.4 %all_gather.12 = bf16[2,64,1024]{2,1,0:T(8,128)(2,1)} all-gather(bf16[2,64,256]{2,1,0:T(8,128)(2,1)S(1)} %reduce_sum.27), channel_id=1, replica_groups=mesh['dp'=8,'tensor'=4,'grid'=16] {'tensor'}, dimensions={2}, use_global_device_ids=true | all-gather | bytes 327680 | tf_op jit(solution)/shard_map/all_gather | solution.py:41
  55.9 40.9 %all-gather.4.cloned.1.call-done = bf16[2,512,1024]{2,1,0:T(8,128)(2,1)} async-done(((bf16[2,64,1024]{2,1,0:T(8,128)(2,1)}), bf16[2,512,1024]{2,1,0:T(8,128)(2,1)}) %all-gather.4.cloned.1.call-update) | async-done | bytes 2097168 | tf_op jit(solution)/shard_map/all_gather | solution.py:42
  96.8 2.6 dynamic-slice_select_fusion
  99.4 0.7 fusion.5
  100.1 1.4 copy.30
  101.5 8.4 %all-to-all-start.2 = ((f32[16,16,2,1024]{3,1,2,0:T(8,128)}), f32[16,16,2,1024]{3,1,2,0:T(8,128)}, u32[]{:S(2)}, u32[]{:S(2)}) async-start(f32[16,16,2,1024]{3,1,2,0:T(8,128)} %copy.30), calls=%async_computation.3 | async-start | bytes 4194304 | tf_op jit(solution)/shard_map/all_to_all | solution.py:18
  110.0 108.0 %reduce-scatter.2.cloned.1.call-done = bf16[32,1024]{1,0:T(8,128)(2,1)} async-done(((bf16[512,1024]{1,0:T(8,128)(2,1)}), bf16[32,1024]{1,0:T(8,128)(2,1)}) %reduce-scatter.2.cloned.1.call-update) | async-done | bytes 65552 | tf_op jit(solution)/shard_map/reduce_scatter | solution.py:34
  218.0 2.4 reduce_sum.29
  220.4 57.0 %all-gather.6.cloned.1.call-done = bf16[512,1024]{1,0:T(8,128)(2,1)} async-done(((bf16[32,1024]{1,0:T(8,128)(2,1)}), bf16[512,1024]{1,0:T(8,128)(2,1)}) %all-gather.6.cloned.1.call-update) | async-done | bytes 1048592 | tf_op jit(solution)/shard_map/all_gather | solution.py:35
  277.4 1.8 fusion.2
  279.3 1.1 copy.29
  280.3 2.7 reshape.27
  283.0 9.3 %all-to-all-start.1 = ((f32[32,1,4096]{2,1,0:T(1,128)}), f32[32,1,4096]{2,1,0:T(1,128)S(1)}, u32[]{:S(2)}, u32[]{:S(2)}) async-start(f32[32,1,4096]{2,1,0:T(1,128)} %reshape.27), calls=%async_computation.2 | async-start | bytes 1048576 | tf_op jit(solution)/shard_map/all_to_all | solution.py:18
  292.4 50.8 %all-gather.8.cloned.1.call-done = f32[256,2,1024]{2,0,1:T(8,128)} async-done(((f32[16,2,1024]{2,0,1:T(8,128)}), f32[256,2,1024]{2,0,1:T(8,128)}) %all-gather.8.cloned.1.call-update) | async-done | bytes 2097168 | tf_op jit(solution)/shard_map/all_gather | solution.py:70
  343.1 2.8 convolution_bitcast_fusion.1
  345.9 0.8 copy.31
  346.8 1.9 reshape.29
  348.6 6.7 %all-to-all-start.3 = ((f32[16,1,2048]{2,1,0:T(1,128)}), f32[16,1,2048]{2,1,0:T(1,128)S(1)}, u32[]{:S(2)}, u32[]{:S(2)}) async-start(f32[16,1,2048]{2,1,0:T(1,128)} %reshape.29), calls=%async_computation.4 | async-start | bytes 262144 | tf_op jit(solution)/shard_map/all_to_all | solution.py:75
  355.4 3.3 fusion
  358.7 0.5 broadcast.2
  359.2 1.8 reduce
  361.0 0.4 reshape.28
  361.5 0.6 multiply_add_fusion
  362.1 3.6 all-to-all-done.3
  365.8 0.9 reduce.1
  366.6 0.2 reshape.30
  366.9 0.1 all_to_all.28
  367.1 0.7 bitcast_add_fusion
  (24 shorter events, 0.6 us)
Async XLA Ops:
  7.2 1.1 copy-start
  7.2 89.6 %all-gather.4.cloned.1.call-start = ((), (), s32[]{:S(2)}) async-start(), calls=%async_computation.5 | async-start | bytes 2359296 | tf_op jit(solution)/shard_map/all_gather | solution.py:42
  49.4 50.0 %copy-start.2 = (bf16[2,256,512]{2,1,0:T(8,128)(2,1)S(1)}, bf16[2,256,512]{2,1,0:T(8,128)(2,1)}, u32[]{:S(2)}) copy-start(bf16[2,256,512]{2,1,0:T(8,128)(2,1)} %param.11) | copy-start | bytes 1572868
  55.8 162.1 %reduce-scatter.2.cloned.1.call-start = ((), (), s32[]{:S(2)}) async-start(), calls=%async_computation.6 | async-start | bytes 1114112 | tf_op jit(solution)/shard_map/reduce_scatter | solution.py:34
  96.8 2.6 copy-start.1
  101.5 116.5 %all-to-all-start.2 = ((f32[16,16,2,1024]{3,1,2,0:T(8,128)}), f32[16,16,2,1024]{3,1,2,0:T(8,128)}, u32[]{:S(2)}, u32[]{:S(2)}) async-start(f32[16,16,2,1024]{3,1,2,0:T(8,128)} %copy.30), calls=%async_computation.3 | async-start | bytes 4194304 | tf_op jit(solution)/shard_map/all_to_all | solution.py:18
  110.0 167.5 %all-gather.6.cloned.1.call-start = ((), (), s32[]{:S(2)}) async-start(), calls=%async_computation.7 | async-start | bytes 1114112 | tf_op jit(solution)/shard_map/all_gather | solution.py:35
  218.0 125.2 %all-gather.8.cloned.1.call-start = ((), (), s32[]{:S(2)}) async-start(), calls=%async_computation.8 | async-start | bytes 2228224 | tf_op jit(solution)/shard_map/all_gather | solution.py:70
  283.0 65.6 %all-to-all-start.1 = ((f32[32,1,4096]{2,1,0:T(1,128)}), f32[32,1,4096]{2,1,0:T(1,128)S(1)}, u32[]{:S(2)}, u32[]{:S(2)}) async-start(f32[32,1,4096]{2,1,0:T(1,128)} %reshape.27), calls=%async_computation.2 | async-start | bytes 1048576 | tf_op jit(solution)/shard_map/all_to_all | solution.py:18
  348.6 17.1 %all-to-all-start.3 = ((f32[16,1,2048]{2,1,0:T(1,128)}), f32[16,1,2048]{2,1,0:T(1,128)S(1)}, u32[]{:S(2)}, u32[]{:S(2)}) async-start(f32[16,1,2048]{2,1,0:T(1,128)} %reshape.29), calls=%async_computation.4 | async-start | bytes 262144 | tf_op jit(solution)/shard_map/all_to_all | solution.py:75
  358.7 2.9 copy-start.4
  361.0 6.1 %copy-start.3 = (f32[2,16,1024]{2,1,0:T(8,128)S(1)}, f32[2,16,1024]{2,1,0:T(8,128)}, u32[]{:S(2)}) copy-start(f32[2,16,1024]{2,1,0:T(8,128)} %param.13) | copy-start | bytes 393220
Sparse Core Ops, SparseCore 0:
  55.9 40.7 all-gather.3
  101.4 116.5 reduce-scatter.1
  221.4 55.9 all-gather.5
  281.3 61.7 all-gather.7
where the time goes:
time: 375 us; the launch traced here: 374 us
  waiting for transfers between devices  260 us (69%)
  blocking collectives  45.2 us (12%)
  starting transfers between devices  24.6 us (7%)
  between operations  14 us (4%)
  local copies, waits for them, and re-layouts  10.7 us (3%)
  matrix products  10.4 us (3%)
  other arithmetic  9.07 us (2%)
    reduce_scatter x1, waiting for transfers between devices, spread(): own = lax.psum_scatter(padded, axis, scatter_dimension=0, tiled=True)  108 us
    all_gather x1, waiting for transfers between devices, spread(): lax.all_gather(own, axis, axis=0, tiled=True)[:len(lines)]  57 us
    all_gather x1, waiting for transfers between devices, shards(): lax.all_gather(applied, 'grid', axis=0, tiled=True)  50.8 us
    all_gather x1, waiting for transfers between devices, shards(): grad_rows = lax.all_gather(widened, 'dp', axis=1, tiled=True)  40.9 us
    all_to_all x1, blocking collectives, sum_at_owner(): pieces = lax.all_to_all(in_blocks(shard, dim, size), axis, 0, 0, tiled=True)  38.8 us
    all_to_all x2, starting transfers between devices, sum_at_owner(): pieces = lax.all_to_all(in_blocks(shard, dim, size), axis, 0, 0, tiled=True)  17.8 us
  transfers between devices with their start and end apart: 7, of which 5 were waited for; matrix products, arithmetic and copies ran while one was open for 6% of the time, Pallas kernels for 0%

commit v1 on v0

--- a/solution.py
+++ b/solution.py
@@ -39,7 +39,9 @@
     partial_grad = jnp.einsum("tr,pto->pro", tokens, cotangents, preferred_element_type=jnp.float32)
     shared = sum_at_owner(partial_grad, "dp", 1)
     widened = lax.all_gather(shared.astype(jnp.bfloat16), "tensor", axis=2, tiled=True)
-    grad_rows = lax.all_gather(widened, "dp", axis=1, tiled=True)
+    grad_rows = jnp.concatenate(
+        lax.all_to_all(jnp.stack([widened] * lax.axis_size("dp")), "dp", 0, 0), axis=1
+    )
     block_rows = left_stat.shape[1]
     grid_rows = left_stat.shape[2]
     learner = lax.axis_index("dp") * lax.axis_size("tensor") + lax.axis_index("tensor")

time: 375 us -> 390 us (1.040)
  waiting for transfers between devices: 260 us -> 268 us
  local copies, waits for them, and re-layouts: 10.7 us -> 15.6 us
  starting transfers between devices: 24.6 us -> 28.6 us
    all_to_all x0 -> x1, waiting for transfers between devices: none -> 51.9 us  [shards(): lax.all_to_all(jnp.stack([widened] * lax.axis_size('dp')), 'dp', 0, 0)]
    all_gather x1 -> x0, waiting for transfers between devices: 40.9 us -> none  [shards(): grad_rows = lax.all_gather(widened, 'dp', axis=1, tiled=True)]
where the time goes in v1:
time: 390 us; the launch traced here: 389 us
  waiting for transfers between devices  268 us (69%)
  blocking collectives  44.6 us (11%)
  starting transfers between devices  28.6 us (7%)
  local copies, waits for them, and re-layouts  15.6 us (4%)
  between operations  14 us (4%)
  matrix products  10.4 us (3%)
  other arithmetic  7.81 us (2%)
    reduce_scatter x1, waiting for transfers between devices, spread(): own = lax.psum_scatter(padded, axis, scatter_dimension=0, tiled=True)  105 us
    all_gather x1, waiting for transfers between devices, spread(): lax.all_gather(own, axis, axis=0, tiled=True)[:len(lines)]  57 us
    all_to_all x1, waiting for transfers between devices, shards(): lax.all_to_all(jnp.stack([widened] * lax.axis_size('dp')), 'dp', 0, 0)  51.9 us
    all_gather x1, waiting for transfers between devices, shards(): lax.all_gather(applied, 'grid', axis=0, tiled=True)  50.9 us
    all_to_all x1, blocking collectives, sum_at_owner(): pieces = lax.all_to_all(in_blocks(shard, dim, size), axis, 0, 0, tiled=True)  38.8 us
    all_to_all x2, starting transfers between devices, sum_at_owner(): pieces = lax.all_to_all(in_blocks(shard, dim, size), axis, 0, 0, tiled=True)  18.2 us
  transfers between devices with their start and end apart: 7, of which 5 were waited for; matrix products, arithmetic and copies ran while one was open for 6% of the time, Pallas kernels for 0%

profile of v1, /device:TPU:8, one launch (start us, length us, event | category | flops | bytes accessed | tf_op | source)
XLA Modules:
  0.0 389.0 jit_solution(1158224936518430222)
XLA Ops:
  7.2 1.1 copy-done
  8.3 1.7 convolution_bitcast_fusion
  10.5 38.8 %all_to_all.38 = f32[8,2,64,256]{3,2,1,0:T(8,128)S(1)} all-to-all(f32[8,2,64,256]{3,2,1,0:T(8,128)S(1)} %copy.26), channel_id=1, replica_groups=mesh['dp'=8,'tensor'=4,'grid'=16] {'dp'}, dimensions={0} | all-to-all | bytes 2097152 | tf_op jit(solution)/shard_map/all_to_all | solution.py:18
  49.4 5.8 %all_gather.9 = bf16[2,64,1024]{2,1,0:T(8,128)(2,1)S(1)} all-gather(bf16[2,64,256]{2,1,0:T(8,128)(2,1)S(1)} %reduce_sum.27), channel_id=1, replica_groups=mesh['dp'=8,'tensor'=4,'grid'=16] {'tensor'}, dimensions={2}, use_global_device_ids=true | all-gather | bytes 327680 | tf_op jit(solution)/shard_map/all_gather | solution.py:41
  55.2 1.6 stack.2
  56.8 3.6 all-to-all-start.1
  60.5 51.9 %all-to-all-done.1 = bf16[8,2,64,1024]{3,2,1,0:T(8,128)(2,1)S(1)} async-done(((bf16[8,2,64,1024]{3,2,1,0:T(8,128)(2,1)}), bf16[8,2,64,1024]{3,2,1,0:T(8,128)(2,1)S(1)}, u32[]{:S(2)}, u32[]{:S(2)}) %all-to-all-start.1) | async-done | bytes 2097184 | tf_op jit(solution)/shard_map/all_to_all | solution.py:43
  112.4 1.3 copy-done.1
  113.7 1.8 copy.27
  115.6 1.2 dynamic-slice_select_fusion
  116.8 0.7 fusion.5
  117.5 1.4 copy.31
  118.9 8.8 %all-to-all-start.3 = ((f32[16,16,2,1024]{3,1,2,0:T(8,128)}), f32[16,16,2,1024]{3,1,2,0:T(8,128)}, u32[]{:S(2)}, u32[]{:S(2)}) async-start(f32[16,16,2,1024]{3,1,2,0:T(8,128)} %copy.31), calls=%async_computation.4 | async-start | bytes 4194304 | tf_op jit(solution)/shard_map/all_to_all | solution.py:18
  127.8 104.7 %reduce-scatter.2.cloned.1.call-done = bf16[32,1024]{1,0:T(8,128)(2,1)} async-done(((bf16[512,1024]{1,0:T(8,128)(2,1)}), bf16[32,1024]{1,0:T(8,128)(2,1)}) %reduce-scatter.2.cloned.1.call-update) | async-done | bytes 65552 | tf_op jit(solution)/shard_map/reduce_scatter | solution.py:34
  232.6 2.4 reduce_sum.29
  235.0 57.0 %all-gather.3.cloned.1.call-done = bf16[512,1024]{1,0:T(8,128)(2,1)} async-done(((bf16[32,1024]{1,0:T(8,128)(2,1)}), bf16[512,1024]{1,0:T(8,128)(2,1)}) %all-gather.3.cloned.1.call-update) | async-done | bytes 1048592 | tf_op jit(solution)/shard_map/all_gather | solution.py:35
  292.0 1.8 fusion.2
  293.9 1.1 copy.30
  295.0 2.7 reshape.37
  297.6 9.3 %all-to-all-start.2 = ((f32[32,1,4096]{2,1,0:T(1,128)}), f32[32,1,4096]{2,1,0:T(1,128)S(1)}, u32[]{:S(2)}, u32[]{:S(2)}) async-start(f32[32,1,4096]{2,1,0:T(1,128)} %reshape.37), calls=%async_computation.3 | async-start | bytes 1048576 | tf_op jit(solution)/shard_map/all_to_all | solution.py:18
  307.0 50.9 %all-gather.5.cloned.1.call-done = f32[256,2,1024]{2,0,1:T(8,128)} async-done(((f32[16,2,1024]{2,0,1:T(8,128)}), f32[256,2,1024]{2,0,1:T(8,128)}) %all-gather.5.cloned.1.call-update) | async-done | bytes 2097168 | tf_op jit(solution)/shard_map/all_gather | solution.py:72
  357.9 2.8 convolution_bitcast_fusion.1
  360.6 0.8 copy.32
  361.5 1.9 reshape.39
  363.4 6.7 %all-to-all-start.4 = ((f32[16,1,2048]{2,1,0:T(1,128)}), f32[16,1,2048]{2,1,0:T(1,128)S(1)}, u32[]{:S(2)}, u32[]{:S(2)}) async-start(f32[16,1,2048]{2,1,0:T(1,128)} %reshape.39), calls=%async_computation.5 | async-start | bytes 262144 | tf_op jit(solution)/shard_map/all_to_all | solution.py:77
  370.1 3.3 fusion
  373.4 0.5 broadcast.4
  373.9 1.9 reduce
  376.3 0.6 multiply_add_fusion
  376.9 3.5 all-to-all-done.4
  380.5 0.9 reduce.1
  381.8 0.7 bitcast_add_fusion
  (25 shorter events, 1.6 us)
Async XLA Ops:
  7.2 1.1 copy-start
  56.8 55.6 %all-to-all-start.1 = ((bf16[8,2,64,1024]{3,2,1,0:T(8,128)(2,1)}), bf16[8,2,64,1024]{3,2,1,0:T(8,128)(2,1)S(1)}, u32[]{:S(2)}, u32[]{:S(2)}) async-start(bf16[8,2,64,1024]{3,2,1,0:T(8,128)(2,1)} %stack.2), calls=%async_computation.1 | async-start | bytes 4194304 | tf_op jit(solution)/shard_map/all_to_all | solution.py:43
  60.4 172.2 %reduce-scatter.2.cloned.1.call-start = ((), (), s32[]{:S(2)}) async-start(), calls=%async_computation.6 | async-start | bytes 1114112 | tf_op jit(solution)/shard_map/reduce_scatter | solution.py:34
  112.4 1.3 copy-start.1
  115.5 1.2 copy-start.2
  118.9 113.7 %all-to-all-start.3 = ((f32[16,16,2,1024]{3,1,2,0:T(8,128)}), f32[16,16,2,1024]{3,1,2,0:T(8,128)}, u32[]{:S(2)}, u32[]{:S(2)}) async-start(f32[16,16,2,1024]{3,1,2,0:T(8,128)} %copy.31), calls=%async_computation.4 | async-start | bytes 4194304 | tf_op jit(solution)/shard_map/all_to_all | solution.py:18
  127.8 164.3 %all-gather.3.cloned.1.call-start = ((), (), s32[]{:S(2)}) async-start(), calls=%async_computation.7 | async-start | bytes 1114112 | tf_op jit(solution)/shard_map/all_gather | solution.py:35
  232.6 125.3 %all-gather.5.cloned.1.call-start = ((), (), s32[]{:S(2)}) async-start(), calls=%async_computation.8 | async-start | bytes 2228224 | tf_op jit(solution)/shard_map/all_gather | solution.py:72
  297.6 65.7 %all-to-all-start.2 = ((f32[32,1,4096]{2,1,0:T(1,128)}), f32[32,1,4096]{2,1,0:T(1,128)S(1)}, u32[]{:S(2)}, u32[]{:S(2)}) async-start(f32[32,1,4096]{2,1,0:T(1,128)} %reshape.37), calls=%async_computation.3 | async-start | bytes 1048576 | tf_op jit(solution)/shard_map/all_to_all | solution.py:18
  363.4 17.1 %all-to-all-start.4 = ((f32[16,1,2048]{2,1,0:T(1,128)}), f32[16,1,2048]{2,1,0:T(1,128)S(1)}, u32[]{:S(2)}, u32[]{:S(2)}) async-start(f32[16,1,2048]{2,1,0:T(1,128)} %reshape.39), calls=%async_computation.5 | async-start | bytes 262144 | tf_op jit(solution)/shard_map/all_to_all | solution.py:77
  373.4 2.9 copy-start.4
  375.8 6.1 %copy-start.3 = (f32[2,16,1024]{2,1,0:T(8,128)S(1)}, f32[2,16,1024]{2,1,0:T(8,128)}, u32[]{:S(2)}) copy-start(f32[2,16,1024]{2,1,0:T(8,128)} %param.13) | copy-start | bytes 393220
Sparse Core Ops, SparseCore 0:
  116.9 115.6 reduce-scatter.1
  236.0 56.0 all-gather.2
  296.1 61.7 all-gather.4
